TPU v7x, 512 devices: a whole 4x8x8 slice. The times are simulated.
512 devices in a mesh: wide: 64 (over y, x, core), narrow: 8 (over z).
Axes of the slice: x: 4, y: 8, z: 8, core: 2. Of those that a mesh axis runs over, the one named last changes fastest.
Arguments:
- momentum: bfloat16 [16384, 16384], P('wide', 'narrow'), may hold values from -16 to 16
- basis: bfloat16 [8, 2048, 256], P('narrow', 'wide'), may hold values from -0.046875 to 0.046875
Outputs:
- momentum_new: float32 [16384, 16384], P('wide', 'narrow')
- direction: bfloat16 [16384, 16384], P('wide', 'narrow')
- basis_new: bfloat16 [8, 2048, 256], P('narrow', 'wide')
All inputs are finite; a program needn't handle non-finite values.
Results may differ from a plain program's by a relative error of at most 0.015.
Values may be sent and summed in bfloat16 or wider, within the bound.
A program may use at most 64 MiB of HBM per device.

v0:
```python
import math

import jax
import jax.numpy as jnp
from jax import lax
from jax.sharding import PartitionSpec as P

M_ROWS = 16384
N = 16384
R = 256
ITERS = 2


def whiten(summed, gram_matrix):
    factor = jnp.linalg.cholesky(gram_matrix)
    return lax.linalg.triangular_solve(
        factor, summed, left_side=False, lower=True, transpose_a=True
    ).astype(jnp.bfloat16)


def orthonormal(partial_value):
    summed = lax.psum(partial_value, "narrow")
    gram_part = jnp.dot(summed.T, summed, precision=lax.Precision.HIGHEST)
    gram_matrix = lax.psum(gram_part, "wide")
    return whiten(summed, gram_matrix)


def on_device(momentum, basis):
    rank_width = basis.shape[2]
    own_count = basis.shape[1]
    q_rows = basis.reshape(own_count, rank_width)
    contract = (((0,), (0,)), ((), ()))
    for iteration in range(ITERS):
        q_block = lax.all_gather(q_rows, "wide", axis=0, tiled=True)
        partial_value = jnp.dot(momentum, q_block, preferred_element_type=jnp.float32)
        left_basis = orthonormal(partial_value)
        last_turn = iteration == ITERS - 1
        right_rows = lax.psum_scatter(
            lax.dot_general(momentum, left_basis, contract, preferred_element_type=jnp.float32),
            "wide",
            scatter_dimension=0,
            tiled=True,
        )
        squares = lax.psum(jnp.sum(right_rows * right_rows, axis=0), ("wide", "narrow"))
        q_rows = (right_rows / jnp.sqrt(squares + 1e-06)).astype(jnp.bfloat16)
        if last_turn:
            right_low, q_block = (
                lax.all_gather(right_rows.astype(jnp.bfloat16), "wide", axis=0, tiled=True),
                lax.all_gather(q_rows, "wide", axis=0, tiled=True),
            )
    outer = (((1,), (1,)), ((), ()))
    feedback = lax.dot_general(left_basis, right_low, outer, preferred_element_type=jnp.float32)
    momentum_new = momentum.astype(jnp.float32) - 0.05 * feedback
    scaling = 0.25 * math.sqrt(M_ROWS * N / R)
    product = lax.dot_general(left_basis, q_block, outer, preferred_element_type=jnp.float32)
    direction = (scaling * product).astype(jnp.bfloat16)
    return (momentum_new, direction, q_rows.reshape(1, own_count, rank_width))


def solution(mesh):
    placed = (P("wide", "narrow"), P("narrow", "wide", None))
    return jax.shard_map(
        on_device,
        mesh=mesh,
        in_specs=placed,
        out_specs=(P("wide", "narrow"), P("wide", "narrow"), P("narrow", "wide", None)),
        check_vma=False,
    )
```

profile of v0, /device:TPU:1, one launch (start us, length us, event | category | flops | bytes accessed | tf_op | source)
XLA Modules:
  0.0 1505.0 jit_solution(5934508107596023184)
XLA Ops:
  7.2 0.7 all-gather.12.cloned.1.call-update
  7.9 90.9 %all-gather.12.cloned.1.call-done = bf16[1,2048,256]{2,1,0:T(8,128)(2,1)} async-done(((bf16[1,32,256]{2,1,0:T(8,128)(2,1)}), bf16[1,2048,256]{2,1,0:T(8,128)(2,1)}) %all-gather.12.cloned.1.call-update) | async-done | bytes 1048592 | tf_op jit(solution)/shard_map/all_gather | solution.py:34
  98.8 2.7 fusion.2
  101.6 71.9 %all-reduce.6.cloned.1.call-done = f32[256,256]{1,0:T(8,128)} async-done(((f32[256,256]{1,0:T(8,128)}), f32[256,256]{1,0:T(8,128)}) %all-reduce.6.cloned.1.call-update) | async-done | bytes 262160 | tf_op jit(solution)/shard_map/psum | solution.py:22
  173.4 2.3 fusion.27
  175.8 191.4 %all-reduce.8.cloned.1.call-done = f32[256,256]{0,1:T(8,128)} async-done(((f32[256,256]{0,1:T(8,128)}), f32[256,256]{0,1:T(8,128)}) %all-reduce.8.cloned.1.call-update) | async-done | bytes 262160 | tf_op jit(solution)/shard_map/psum | solution.py:24
  367.2 1.1 copy.19
  368.3 1.0 fusion.5
  369.3 11.7 cholesky.130
  381.1 9.8 custom-call.13
  390.9 0.2 constant_dynamic-update-slice_fusion.3
  391.2 0.3 convolution_subtract_fusion.3
  391.4 11.7 cholesky.147
  403.2 0.6 compare_reduce_fusion.2
  405.2 4.2 while.4
  405.4 0.6 fusion.51
  406.0 1.4 bitcast_dynamic-update-slice_fusion.4
  407.4 0.6 fusion.51
  408.0 1.4 bitcast_dynamic-update-slice_fusion.4
  409.4 19.7 %custom-call.14 = f32[2,128,128]{1,2,0:T(8,128)S(1)} custom-call(f32[2,128,128]{2,1,0:T(8,128)S(1)} %get-tuple-element.19), custom_call_target="InvertDiagBlocksLowerTriangular" | custom-call | tf_op jit(solution)/shard_map/triangular_solve/custom-call.0 | solution.py:16
  429.1 0.3 fusion.8
  429.4 0.4 convolution_subtract_fusion.1
  429.8 0.3 fusion.14
  430.2 0.4 convolution_bitcast_fusion.1
  430.6 1.8 copy.30
  432.5 141.2 %reduce-scatter.7.cloned.1.call-done = f32[32,256]{1,0:T(8,128)} async-done(((f32[2048,256]{1,0:T(8,128)}), f32[32,256]{1,0:T(8,128)}) %reduce-scatter.7.cloned.1.call-update) | async-done | bytes 32784 | tf_op jit(solution)/shard_map/reduce_scatter | solution.py:38
  573.7 0.9 copy.31
  574.7 101.9 %psum.44 = f32[256]{0:T(256)S(1)} all-reduce(f32[256]{0:T(256)S(1)} %multiply_reduce_fusion.1), channel_id=1, replica_groups=mesh['wide'=64,'narrow'=8] {'wide','narrow'}, use_global_device_ids=true, to_apply=%region_8.11 | all-reduce | flops 256 | bytes 2048 | tf_op jit(solution)/shard_map/psum | solution.py:44
  676.6 1.4 divide_convert_fusion.1
  678.1 77.5 %all-gather.6.cloned.1.call-done = bf16[2048,256]{1,0:T(8,128)(2,1)} async-done(((bf16[32,256]{1,0:T(8,128)(2,1)}), bf16[2048,256]{1,0:T(8,128)(2,1)}) %all-gather.6.cloned.1.call-update) | async-done | bytes 1048592 | tf_op jit(solution)/shard_map/all_gather | solution.py:34
  755.6 2.4 convolution_bitcast_fusion.2
  758.0 72.1 %all-reduce.10.cloned.1.call-done = f32[256,256]{0,1:T(8,128)} async-done(((f32[256,256]{0,1:T(8,128)}), f32[256,256]{0,1:T(8,128)}) %all-reduce.10.cloned.1.call-update) | async-done | bytes 262160 | tf_op jit(solution)/shard_map/psum | solution.py:22
  830.1 2.1 fusion.28
  832.4 191.2 %all-reduce.12.cloned.1.call-done = f32[256,256]{0,1:T(8,128)} async-done(((f32[256,256]{0,1:T(8,128)}), f32[256,256]{0,1:T(8,128)}) %all-reduce.12.cloned.1.call-update) | async-done | bytes 262160 | tf_op jit(solution)/shard_map/psum | solution.py:24
  1023.6 1.1 copy.22
  1024.7 1.0 fusion.4
  1025.7 11.7 cholesky.164
  1037.4 0.6 compare_reduce_fusion.1
  1038.1 9.8 custom-call.15
  1047.9 0.2 constant_dynamic-update-slice_fusion.1
  1048.1 0.3 convolution_subtract_fusion.2
  1048.4 11.7 cholesky.181
  1060.1 0.6 compare_reduce_fusion
  1062.1 4.2 while.5
  1062.4 0.6 fusion.52
  1063.0 1.4 bitcast_dynamic-update-slice_fusion.5
  1064.4 0.6 fusion.52
  1065.0 1.4 bitcast_dynamic-update-slice_fusion.5
  1066.4 19.7 %custom-call.16 = f32[2,128,128]{1,2,0:T(8,128)S(1)} custom-call(f32[2,128,128]{2,1,0:T(8,128)S(1)} %get-tuple-element.20), custom_call_target="InvertDiagBlocksLowerTriangular" | custom-call | tf_op jit(solution)/shard_map/triangular_solve/custom-call.0 | solution.py:16
  1086.0 0.3 fusion.6
  1086.4 0.3 convolution_subtract_fusion
  1086.6 0.3 fusion.10
  1087.0 0.4 convolution_bitcast_fusion
  1087.4 1.8 copy.32
  1089.3 141.3 %reduce-scatter.9.cloned.1.call-done = f32[32,256]{1,0:T(8,128)} async-done(((f32[2048,256]{1,0:T(8,128)}), f32[32,256]{1,0:T(8,128)}) %reduce-scatter.9.cloned.1.call-update) | async-done | bytes 32784 | tf_op jit(solution)/shard_map/reduce_scatter | solution.py:38
  1230.6 0.9 copy.33
  1231.5 101.9 %psum.47 = f32[256]{0:T(256)S(1)} all-reduce(f32[256]{0:T(256)S(1)} %multiply_reduce_fusion), channel_id=1, replica_groups=mesh['wide'=64,'narrow'=8] {'wide','narrow'}, use_global_device_ids=true, to_apply=%region_13.16 | all-reduce | flops 256 | bytes 2048 | tf_op jit(solution)/shard_map/psum | solution.py:44
  1333.6 0.7 copy.25
  1334.3 1.4 convert_element_type.25
  1335.9 0.7 copy.26
  1336.5 75.2 %all-gather.10.cloned.1.call-done = bf16[2048,256]{1,0:T(8,128)(2,1)} async-done(((bf16[32,256]{1,0:T(8,128)(2,1)}), bf16[2048,256]{1,0:T(8,128)(2,1)}) %all-gather.10.cloned.1.call-update) | async-done | bytes 1048592 | tf_op jit(solution)/shard_map/all_gather | solution.py:49
  1411.7 2.7 fusion.1
  1414.4 80.7 %all-gather.8.cloned.1.call-done = bf16[2048,256]{1,0:T(8,128)(2,1)} async-done(((bf16[32,256]{1,0:T(8,128)(2,1)}), bf16[2048,256]{1,0:T(8,128)(2,1)}) %all-gather.8.cloned.1.call-update) | async-done | bytes 1048592 | tf_op jit(solution)/shard_map/all_gather | solution.py:48
  1495.1 3.0 fusion
  (49 shorter events, 1.4 us)
Async XLA Ops:
  7.2 91.6 %all-gather.12.cloned.1.call-start = ((), (), s32[]{:S(2)}) async-start(), calls=%async_computation.9 | async-start | bytes 1064960 | tf_op jit(solution)/shard_map/all_gather | solution.py:34
  7.9 165.5 %all-reduce.6.cloned.1.call-start = ((), (), s32[]{:S(2)}) async-start(), calls=%async_computation.2 | async-start | bytes 524288 | tf_op jit(solution)/shard_map/psum | solution.py:22
  101.5 265.7 %all-reduce.8.cloned.1.call-start = ((), (), s32[]{:S(2)}) async-start(), calls=%async_computation.3 | async-start | bytes 524288 | tf_op jit(solution)/shard_map/psum | solution.py:24
  175.8 253.3 %copy-start.1 = (f32[256,256]{1,0:T(8,128)S(1)}, f32[256,256]{1,0:T(8,128)}, u32[]{:S(2)}) copy-start(f32[256,256]{1,0:T(8,128)} %all-reduce.6.cloned.1.call-done) | copy-start | bytes 786436
  175.8 398.0 %reduce-scatter.7.cloned.1.call-start = ((), (), s32[]{:S(2)}) async-start(), calls=%async_computation.10 | async-start | bytes 2129920 | tf_op jit(solution)/shard_map/reduce_scatter | solution.py:38
  369.3 60.8 %copy-start = (bf16[256,2048]{1,0:T(8,128)(2,1)S(1)}, bf16[256,2048]{1,0:T(8,128)(2,1)}, u32[]{:S(2)}) copy-start(bf16[256,2048]{1,0:T(8,128)(2,1)} %param.5) | copy-start | bytes 3145732
  432.4 323.1 %all-gather.6.cloned.1.call-start = ((), (), s32[]{:S(2)}) async-start(), calls=%async_computation.4 | async-start | bytes 1064960 | tf_op jit(solution)/shard_map/all_gather | solution.py:34
  678.0 152.1 %all-reduce.10.cloned.1.call-start = ((), (), s32[]{:S(2)}) async-start(), calls=%async_computation.5 | async-start | bytes 524288 | tf_op jit(solution)/shard_map/psum | solution.py:22
  758.0 265.6 %all-reduce.12.cloned.1.call-start = ((), (), s32[]{:S(2)}) async-start(), calls=%async_computation.6 | async-start | bytes 524288 | tf_op jit(solution)/shard_map/psum | solution.py:24
  832.3 253.7 %copy-start.2 = (f32[256,256]{0,1:T(8,128)S(1)}, f32[256,256]{0,1:T(8,128)}, u32[]{:S(2)}) copy-start(f32[256,256]{0,1:T(8,128)} %all-reduce.10.cloned.1.call-done) | copy-start | bytes 786436
  832.3 398.2 %reduce-scatter.9.cloned.1.call-start = ((), (), s32[]{:S(2)}) async-start(), calls=%async_computation.11 | async-start | bytes 2129920 | tf_op jit(solution)/shard_map/reduce_scatter | solution.py:38
  1089.2 322.5 %all-gather.10.cloned.1.call-start = ((), (), s32[]{:S(2)}) async-start(), calls=%async_computation.8 | async-start | bytes 1064960 | tf_op jit(solution)/shard_map/all_gather | solution.py:49
  1334.3 160.8 %all-gather.8.cloned.1.call-start = ((), (), s32[]{:S(2)}) async-start(), calls=%async_computation.7 | async-start | bytes 1064960 | tf_op jit(solution)/shard_map/all_gather | solution.py:48
Sparse Core Ops, SparseCore 0:
  11.3 87.4 all-gather.11
  101.7 71.6 all-reduce.5
  177.9 189.3 all-reduce.7
  432.6 141.1 reduce-scatter.6
  678.2 77.3 all-gather.5
  758.4 71.6 all-reduce.9
  834.2 189.3 all-reduce.11
  1089.4 141.1 reduce-scatter.8
  1334.4 77.2 all-gather.9
  1415.5 79.5 all-gather.7
where the time goes:
time: 1510 us; the launch traced here: 1500 us
  waiting for transfers between devices  1130 us (75%)
  blocking collectives  204 us (14%)
  other arithmetic  113 us (7%)
  matrix products  19 us (1%)
  between operations  17.1 us (1%)
  local copies, waits for them, and re-layouts  16.9 us (1%)
    psum x2, waiting for transfers between devices, orthonormal(): gram_matrix = lax.psum(gram_part, 'wide')  383 us
    reduce_scatter x2, waiting for transfers between devices, on_device(): lax.psum_scatter(lax.dot_general(momentum, left_basis, contract, preferre...  283 us
    psum x2, blocking collectives, on_device(): lax.psum(jnp.sum(right_rows * right_rows, axis=0), ('wide', 'narrow'))  204 us
    all_gather x2, waiting for transfers between devices, on_device(): q_block = lax.all_gather(q_rows, 'wide', axis=0, tiled=True)  168 us
    psum x2, waiting for transfers between devices, orthonormal(): summed = lax.psum(partial_value, 'narrow')  144 us
    all_gather x1, waiting for transfers between devices, on_device(): lax.all_gather(right_rows.astype(jnp.bfloat16), 'wide', axis=0, tiled=True)  80.7 us
    all_gather x1, waiting for transfers between devices, on_device(): lax.all_gather(q_rows, 'wide', axis=0, tiled=True)  75.2 us
    another operation x13, other arithmetic, whiten(): factor = jnp.linalg.cholesky(gram_matrix)  68.5 us
  transfers between devices with their start and end apart: 10, of which 10 were waited for; matrix products, arithmetic and copies ran while one was open for 0% of the time, Pallas kernels for 0%

commit v1 on v0

v1 whole, which is shorter than its diff:
```python
import functools
import math

import jax
import jax.numpy as jnp
from jax import lax
from jax.experimental import pallas as pl
from jax.experimental.pallas import tpu as pltpu
from jax.sharding import PartitionSpec as P

M_ROWS = 16384
N = 16384
R = 256
ITERS = 2
NC = 2
NX = 4
LEAF = 64
GROUP = 16
QUAD = 4
F32 = jnp.float32
BF16 = jnp.bfloat16
HIGHEST = lax.Precision.HIGHEST


def far_first(count):
    return sorted(range(1, count), key=lambda d: -min(d, count - d))


def dot_t(a, b):
    return lax.dot_general(a, b, (((1,), (1,)), ((), ())), preferred_element_type=F32, precision=HIGHEST)


def leaf_inverse(block):
    rows = lax.broadcasted_iota(jnp.int32, (LEAF, 2 * LEAF), 0)
    lanes = lax.broadcasted_iota(jnp.int32, (LEAF, 2 * LEAF), 1)
    eye = jnp.where(lanes == rows + LEAF, 1.0, 0.0).astype(F32)
    work = jnp.where(lanes < LEAF, jnp.concatenate([block, block], axis=1), eye)

    def group(step, work):
        alive = rows < LEAF - GROUP * step
        for first in range(0, GROUP, QUAD):
            cols = [jnp.broadcast_to(work[:, first + k : first + k + 1], (LEAF, 2 * LEAF)) for k in range(QUAD)]
            pivot_rows = [work[first + k : first + k + 1, :] for k in range(QUAD)]
            update = None
            for k in range(QUAD):
                at = first + k
                inverse = 1.0 / cols[k][at : at + 1, :]
                scaled = pivot_rows[k] * inverse
                for later in range(k + 1, QUAD):
                    ratio = cols[k][first + later : first + later + 1, :] * inverse
                    cols[later] = cols[later] - cols[k] * ratio
                    pivot_rows[later] = pivot_rows[later] - ratio * pivot_rows[k]
                term = jnp.where(alive & (rows > at), cols[k], 0.0) * scaled
                update = term if update is None else update + term
            work = work - update
        work = jnp.concatenate([work[GROUP:], work[:GROUP]], axis=0)
        return pltpu.roll(work, 2 * LEAF - GROUP, 1)

    work = lax.fori_loop(0, LEAF // GROUP, group, work)
    diagonal = jnp.sum(jnp.where(lanes == rows + LEAF, work, 0.0), axis=1, keepdims=True)
    return work[:, :LEAF] * (1.0 / jnp.sqrt(diagonal))


def inverse_factor(gram, work, inverse):
    work[...] = gram
    rows = lax.broadcasted_iota(jnp.int32, (R, R), 0)
    lanes = lax.broadcasted_iota(jnp.int32, (R, R), 1)
    inverse[...] = jnp.where(rows == lanes, 1.0, 0.0).astype(F32)
    for start in range(0, R, LEAF):
        stop = start + LEAF
        leaf = leaf_inverse(work[start:stop, start:stop])
        own = jnp.dot(leaf, inverse[start:stop, :], preferred_element_type=F32, precision=HIGHEST)
        inverse[start:stop, :] = own
        if stop < R:
            panel = jnp.dot(leaf, work[start:stop, :], preferred_element_type=F32, precision=HIGHEST)
            below = jnp.transpose(panel)[stop:, :]
            work[stop:, :] = work[stop:, :] - jnp.dot(below, panel, preferred_element_type=F32, precision=HIGHEST)
            inverse[stop:, :] = inverse[stop:, :] - jnp.dot(below, own, preferred_element_type=F32, precision=HIGHEST)


def kernel(sizes, m_ref, q_ref, left_out, right_out, norms_out, rows_out, mt, gathered, partial, partial_low, core_in, core_sum, x_in,
           x_low, y_in, z_out, z_in, z_all, square_all, g_out, g_core, g_sum, g_x, g_y_out, g_y_in, g_all, work, inverse, send, recv):
    ny, nz, block, tall = sizes
    w = lax.axis_index("wide")
    z = lax.axis_index("narrow")
    c, x, y = w % NC, (w // NC) % NX, w // (NC * NX)
    strip = tall // nz

    def core_peer():
        return {"wide": (y * NX + x) * NC + (1 - c)}

    def x_peer(d):
        return (x + d) % NX, {"wide": (y * NX + (x + d) % NX) * NC + c}

    def y_peer(d):
        return (y + d) % ny, {"wide": (((y + d) % ny) * NX + x) * NC + c}

    def z_peer(d):
        return (z + d) % nz, {"narrow": (z + d) % nz}

    barrier = pltpu.get_barrier_semaphore()
    peers = [core_peer()] + [x_peer(d)[1] for d in range(1, NX)] + [y_peer(d)[1] for d in range(1, ny)]
    peers += [z_peer(d)[1] for d in range(1, nz)]
    for peer in peers:
        pl.semaphore_signal(barrier, inc=1, device_id=peer, device_id_type=pl.DeviceIdType.MESH)
    pl.semaphore_wait(barrier, len(peers))

    sent = []

    def push(src, dst, peer):
        at = len(sent)
        copy = pltpu.make_async_remote_copy(src_ref=src, dst_ref=dst, send_sem=send.at[at], recv_sem=recv.at[at], device_id=peer,
                                            device_id_type=pl.DeviceIdType.MESH)
        copy.start()
        sent.append(copy)
        return copy

    def gather_plane(buf, beside=None):
        first = {d: push(buf.at[y, x, c], buf.at[y, x, c], y_peer(d)[1]) for d in far_first(ny)}
        if beside is not None:
            beside()
        for d in first:
            first[d].wait_recv()
        second = {d: push(buf.at[:, x, c], buf.at[:, x, c], x_peer(d)[1]) for d in far_first(NX)}
        third = [push(buf.at[:, x, c], buf.at[:, x, c], core_peer())]
        for d in sorted(second, key=lambda d: min(d, NX - d)):
            second[d].wait_recv()
            came = (x + NX - d) % NX
            third.append(push(buf.at[:, came, c], buf.at[:, came, c], core_peer()))
        for copy in third:
            copy.wait_recv()

    def exchange_narrow(buf):
        copies = [push(buf.at[z], buf.at[z], z_peer(d)[1]) for d in far_first(nz)]
        for copy in copies:
            copy.wait_recv()

    def transpose_momentum():
        def one(k, carry):
            at = pl.multiple_of(k * 256, 256)
            mt[pl.ds(at, 256), :] = jnp.transpose(m_ref[:, pl.ds(at, 256)])
            return carry

        lax.fori_loop(0, mt.shape[0] // 256, one, 0)

    def product(t):
        def one(k, total):
            at = pl.multiple_of(k * NX * NC * block, 256)
            q_part = gathered[t, k].reshape(NX * NC * block, R)
            return total + jnp.dot(m_ref[:, pl.ds(at, NX * NC * block)], q_part, preferred_element_type=F32)

        return lax.fori_loop(0, ny, one, jnp.zeros((tall, R), F32))

    def squares(t):
        def one(k, total):
            part = gathered[t, k].astype(F32).reshape(NX * NC * block, R)
            return total + jnp.sum((part * part).reshape(-1, 8, R), axis=0)

        total = lax.fori_loop(0, ny, one, jnp.zeros((8, R), F32))
        square_all[t, z] = total

    def norms(t):
        total = jnp.sum(square_all[t].reshape(nz * 8, R), axis=0, keepdims=True)
        return jnp.sqrt(total + 1e-06)

    def reduce_narrow(t, scale):
        copies = [push(z_out.at[t, z_peer(d)[0]], z_in.at[t, d - 1], z_peer(d)[1]) for d in far_first(nz)]
        total = z_out[t, z]
        for copy in copies:
            copy.wait_recv()
        for d in range(1, nz):
            total = total + z_in[t, d - 1]
        z_all[t, z] = total * scale() if scale is not None else total
        exchange_narrow(z_all.at[t])

    def reduce_gram(t):
        other = pl.ds(pl.multiple_of((1 - c) * (R // NC), 8), R // NC)
        mine = pl.ds(pl.multiple_of(c * (R // NC), 8), R // NC)
        push(g_out.at[t, other], g_core.at[t], core_peer()).wait_recv()
        g_sum[t] = (g_out[t, mine, :] + g_core[t]).reshape(NX, R // NC // NX, R)
        copies = [push(g_sum.at[t, x_peer(d)[0]], g_x.at[t, d - 1], x_peer(d)[1]) for d in far_first(NX)]
        total = g_sum[t, x]
        for copy in copies:
            copy.wait_recv()
        for d in range(1, NX):
            total = total + g_x[t, d - 1]
        total = total.reshape(ny // 2, -1, R)
        g_y_out[t, :, 0] = total[:, :, : R // 2]
        g_y_out[t, :, 1] = total[:, :, R // 2 :]
        copies = []
        for d in far_first(ny):
            to, peer = y_peer(d)
            copies.append(push(g_y_out.at[t, to // 2, to % 2], g_y_in.at[t, d - 1], peer))
        total = g_y_out[t, y // 2, y % 2]
        for copy in copies:
            copy.wait_recv()
        for d in range(1, ny):
            total = total + g_y_in[t, d - 1]
        mine = g_all.at[t, c, x, y // 2, y % 2]
        mine[...] = total
        copies = [push(mine, mine, y_peer(d)[1]) for d in far_first(ny)]
        for copy in copies:
            copy.wait_recv()
        mine = g_all.at[t, c, x]
        copies = [push(mine, mine, x_peer(d)[1]) for d in far_first(NX)]
        for copy in copies:
            copy.wait_recv()
        mine = g_all.at[t, c]
        push(mine, mine, core_peer()).wait_recv()
        halves = [g_all[t, :, :, :, h].reshape(R, R // 2) for h in range(2)]
        return jnp.concatenate(halves, axis=1)

    def back_product(t, left):
        def one(k, carry):
            at = pl.multiple_of(k * NX * NC * block, 256)
            part = jnp.dot(mt[pl.ds(at, NX * NC * block), :], left, preferred_element_type=F32)
            part = part.reshape(NX, NC, block, R)
            partial[t, k] = part
            partial_low[t, k] = part.astype(BF16)
            return carry

        lax.fori_loop(0, ny, one, 0)
        order = far_first(NX) + [0]
        first = {}
        for d in order:
            to = (x + d) % NX
            first[d] = push(partial_low.at[t, :, to, 1 - c], core_in.at[t, to], core_peer())
        second = []
        for d in order:
            to = (x + d) % NX
            first[d].wait_recv()
            total = partial[t, :, to, c] + core_in[t, to].astype(F32)
            if d:
                core_sum[t, d - 1] = total.astype(BF16)
                second.append(push(core_sum.at[t, d - 1], x_in.at[t, d - 1], x_peer(d)[1]))
        for copy in second:
            copy.wait_recv()
        for d in range(1, NX):
            total = total + x_in[t, d - 1].astype(F32)
        x_low[t] = total.astype(BF16)
        partial[t, :, x, c] = total
        third = [push(x_low.at[t, y_peer(d)[0]], y_in.at[t, d - 1], y_peer(d)[1]) for d in far_first(ny)]
        total = partial[t, y, x, c]
        for copy in third:
            copy.wait_recv()
        for d in range(1, ny):
            total = total + y_in[t, d - 1].astype(F32)
        return total

    gathered[0, y, x, c] = q_ref[...]
    gather_plane(gathered.at[0], transpose_momentum)
    for t in range(ITERS):
        z_out[t] = product(t).reshape(nz, strip, R)
        if t:
            squares(t)
            copies = [push(square_all.at[t, z], square_all.at[t, z], z_peer(d)[1]) for d in far_first(nz)]

            def scale():
                for copy in copies:
                    copy.wait_recv()
                return 1.0 / norms(t)

            reduce_narrow(t, scale)
        else:
            reduce_narrow(t, None)
        summed = z_all[t].reshape(tall, R)
        g_out[t] = jnp.dot(jnp.transpose(summed), summed, preferred_element_type=F32, precision=HIGHEST)
        inverse_factor(reduce_gram(t), work, inverse)
        left = dot_t(z_all[t].reshape(tall, R), inverse[...]).astype(BF16)
        right = back_product(t, left)
        gathered[t + 1, y, x, c] = right.astype(BF16)
        gather_plane(gathered.at[t + 1])
    squares(ITERS)
    exchange_narrow(square_all.at[ITERS])
    last = norms(ITERS)
    norms_out[...] = jnp.broadcast_to(last, (8, R))
    rows_out[...] = (right / last).astype(BF16)
    left_out[...] = left

    def give(k, carry):
        right_out[k] = gathered[ITERS, k].reshape(NX * NC * block, R)
        return carry

    lax.fori_loop(0, ny, give, 0)
    for copy in sent:
        copy.wait_send()


def count_copies(ny, nz):
    xs, ys, zs = NX - 1, ny - 1, nz - 1
    gather = ys + xs + NX
    one = zs + zs + 2 * (1 + xs + ys) + NX + xs + ys
    return (ITERS + 1) * gather + ITERS * one + ITERS * zs


def iterate(mesh, momentum, q_rows):
    ny, nz = mesh.shape["wide"] // (NC * NX), mesh.shape["narrow"]
    tall, broad = momentum.shape
    block = q_rows.shape[0]
    copies = count_copies(ny, nz)
    strip = tall // nz
    g_rows = R // (NC * NX * (ny // 2))
    vmem = pltpu.VMEM
    scratch = [
        vmem((broad, tall), BF16),
        vmem((ITERS + 1, ny, NX, NC, block, R), BF16),
        vmem((ITERS, ny, NX, NC, block, R), F32),
        vmem((ITERS, ny, NX, NC, block, R), BF16),
        vmem((ITERS, NX, ny, block, R), BF16),
        vmem((ITERS, NX - 1, ny, block, R), BF16),
        vmem((ITERS, NX - 1, ny, block, R), BF16),
        vmem((ITERS, ny, block, R), BF16),
        vmem((ITERS, ny - 1, block, R), BF16),
        vmem((ITERS, nz, strip, R), F32),
        vmem((ITERS, nz - 1, strip, R), F32),
        vmem((ITERS, nz, strip, R), F32),
        vmem((ITERS + 1, nz, 8, R), F32),
        vmem((ITERS, R, R), F32),
        vmem((ITERS, R // NC, R), F32),
        vmem((ITERS, NX, R // NC // NX, R), F32),
        vmem((ITERS, NX - 1, R // NC // NX, R), F32),
        vmem((ITERS, ny // 2, 2, g_rows, R // 2), F32),
        vmem((ITERS, ny - 1, g_rows, R // 2), F32),
        vmem((ITERS, NC, NX, ny // 2, 2, g_rows, R // 2), F32),
        vmem((R, R), F32),
        vmem((R, R), F32),
        pltpu.SemaphoreType.DMA((copies,)),
        pltpu.SemaphoreType.DMA((copies,)),
    ]
    whole = pl.BlockSpec(memory_space=pltpu.VMEM)
    return pl.pallas_call(
        functools.partial(kernel, (ny, nz, block, tall)),
        out_shape=(
            jax.ShapeDtypeStruct((tall, R), BF16),
            jax.ShapeDtypeStruct((ny, broad // ny, R), BF16),
            jax.ShapeDtypeStruct((8, R), F32),
            jax.ShapeDtypeStruct((block, R), BF16),
        ),
        in_specs=[whole] * 2,
        out_specs=(whole,) * 4,
        scratch_shapes=scratch,
        compiler_params=pltpu.CompilerParams(collective_id=0, has_side_effects=True, vmem_limit_bytes=48 * 1024 * 1024),
        name="iterate",
    )(momentum, q_rows)


def finish_kernel(scaling, m_ref, left_ref, right_ref, norms_ref, new_ref, direction_ref):
    left = left_ref[...]
    right = right_ref[...]
    outer = (((1,), (1,)), ((), ()))
    feedback = lax.dot_general(left, right, outer, preferred_element_type=F32)
    new_ref[...] = m_ref[...].astype(F32) - 0.05 * feedback
    q_block = (right.astype(F32) / norms_ref[0:1, :]).astype(BF16)
    product = lax.dot_general(left, q_block, outer, preferred_element_type=F32)
    direction_ref[...] = (scaling * product).astype(BF16)


def finish(momentum, left, right, norms):
    tall, broad = momentum.shape
    wide = 512 if broad % 512 == 0 else 256
    scaling = 0.25 * math.sqrt(M_ROWS * N / R)
    return pl.pallas_call(
        functools.partial(finish_kernel, scaling),
        grid=(broad // wide,),
        out_shape=(jax.ShapeDtypeStruct((tall, broad), F32), jax.ShapeDtypeStruct((tall, broad), BF16)),
        in_specs=[
            pl.BlockSpec((tall, wide), lambda j: (0, j)),
            pl.BlockSpec((tall, R), lambda j: (0, 0)),
            pl.BlockSpec((wide, R), lambda j: (j, 0)),
            pl.BlockSpec((8, R), lambda j: (0, 0)),
        ],
        out_specs=(pl.BlockSpec((tall, wide), lambda j: (0, j)), pl.BlockSpec((tall, wide), lambda j: (0, j))),
        name="finish",
    )(momentum, left, right, norms)


def on_device(mesh, momentum, basis):
    q_rows = basis.reshape(basis.shape[1], basis.shape[2])
    left, right, norms, rows = iterate(mesh, momentum, q_rows)
    momentum_new, direction = finish(momentum, left, right.reshape(-1, R), norms)
    return momentum_new, direction, rows.reshape(basis.shape)


def solution(mesh):
    placed = (P("wide", "narrow"), P("narrow", "wide", None))
    return jax.shard_map(
        functools.partial(on_device, mesh),
        mesh=mesh,
        in_specs=placed,
        out_specs=(P("wide", "narrow"), P("wide", "narrow"), P("narrow", "wide", None)),
        check_vma=False,
    )
```

time: 1510 us -> 202 us (0.13)
  waiting for transfers between devices: 1130 us -> 0 us
  blocking collectives: 204 us -> 0 us
  Pallas kernels: 0 us -> 196 us
  other arithmetic: 113 us -> 0 us
  matrix products: 19 us -> 0 us
  between operations: 17.1 us -> 0.66 us
    psum x4 -> x0, waiting for transfers between devices: 527 us -> none  [the longest x2 383 us: orthonormal(): gram_matrix = lax.psum(gram_part, 'wide')]
    all_gather x4 -> x0, waiting for transfers between devices: 324 us -> none  [the longest x2 168 us: on_device(): q_block = lax.all_gather(q_rows, 'wide', axis=0, tiled=True)]
    reduce_scatter x2 -> x0, waiting for transfers between devices: 283 us -> none  [on_device(): lax.psum_scatter(lax.dot_general(momentum, left_basis, contract, preferre...]
    psum x2 -> x0, blocking collectives: 204 us -> none  [on_device(): lax.psum(jnp.sum(right_rows * right_rows, axis=0), ('wide', 'narrow'))]
    pallas_call x0 -> x2, Pallas kernels: none -> 196 us  [the longest x1 192 us: iterate(): pl.pallas_call(functools.partial(kernel, (ny, nz, block, tall)), out_shap...]
    another operation x18 -> x0, other arithmetic: 108 us -> none  [the longest x13 68.5 us: whiten(): factor = jnp.linalg.cholesky(gram_matrix)]
    dot_general x8 -> x0, matrix products: 16.2 us -> none  [the longest x2 5.09 us: on_device(): jnp.dot(momentum, q_block, preferred_element_type=jnp.float32)]
  transfers between devices with their start and end apart: 10 -> 0, of which waited for: 10 -> 0; matrix products, arithmetic and copies ran while one was open for 0% -> 0% of each run, Pallas kernels for 0% -> 0%
where the time goes in v1:
time: 202 us
  Pallas kernels  196 us (97%)
  local copies, waits for them, and re-layouts  4.76 us (2%)
    pallas_call x1, Pallas kernels, iterate(): pl.pallas_call(functools.partial(kernel, (ny, nz, block, tall)), out_shap...  192 us
    unnamed x11, local copies, waits for them, and re-layouts  4.76 us
    pallas_call x1, Pallas kernels, finish(): pl.pallas_call(functools.partial(finish_kernel, scaling), grid=(broad //...  4.43 us

profile of v1, /device:TPU:1, one launch (start us, length us, event | category | flops | bytes accessed | tf_op | source)
XLA Modules:
  0.0 201.7 jit_solution(12399917618218087041)
XLA Ops:
  0.6 0.0 copy-start
  0.6 1.2 copy-done
  1.9 0.0 copy-start.3
  1.9 0.7 copy-done.3
  2.6 191.9 %iterate.1 = (bf16[256,256]{1,0:T(8,128)(2,1)S(1)}, bf16[8,256,256]{2,1,0:T(8,128)(2,1)S(1)}, f32[8,256]{1,0:T(8,128)S(1)}, bf16[32,256]{1,0:T(8,128)(2,1)S(1)}) custom-call(bf16[256,2048]{1,0:T(8,128)(2,1)S(1)} %copy-done, bf16[32,256]{1,0:T(8,128)(2,1)S(1)} %bitcast.4), custom_call_target="tpu_custom_call" | custom-call | tf_op jit(solution)/shard_map/iterate/pallas_call | solution.py:331
  194.5 0.0 copy-start.1
  194.5 1.0 copy-done.1
  195.5 0.0 copy-start.2
  195.5 0.7 copy-done.2
  196.1 0.0 copy-start.4
  196.1 0.6 copy-done.4
  196.7 4.4 %finish.1 = (f32[256,2048]{1,0:T(8,128)}, bf16[256,2048]{1,0:T(8,128)(2,1)}) custom-call(bf16[256,2048]{1,0:T(8,128)(2,1)} %m_ref.3, bf16[256,256]{1,0:T(8,128)(2,1)} %copy-done.2, bf16[2048,256]{1,0:T(8,128)(2,1)} %bitcast.3, f32[8,256]{1,0:T(8,128)} %copy-done.4), custom_call_target="tpu_custom_call" | custom-call | tf_op jit(solution)/shard_map/finish/pallas_call | solution.py:362
  201.1 0.6 copy.6
Async XLA Ops:
  0.6 1.2 copy-start
  1.9 0.7 copy-start.3
  194.5 1.0 copy-start.1
  195.5 0.7 copy-start.2
  196.1 0.6 copy-start.4

commit v2 on v1

--- a/solution.py
+++ b/solution.py
@@ -78,13 +78,16 @@
             inverse[stop:, :] = inverse[stop:, :] - jnp.dot(below, own, preferred_element_type=F32, precision=HIGHEST)
 
 
-def kernel(sizes, m_ref, q_ref, left_out, right_out, norms_out, rows_out, mt, gathered, partial, partial_low, core_in, core_sum, x_in,
-           x_low, y_in, z_out, z_in, z_all, square_all, g_out, g_core, g_sum, g_x, g_y_out, g_y_in, g_all, work, inverse, send, recv):
+def kernel(sizes, m_hbm, q_hbm, left_out, right_out, norms_out, rows_out, m_ref, mt, gathered, partial, partial_low, core_in,
+           core_sum, x_far, x_in, x_low, y_in, z_out, z_in, z_all, square_all, g_out, g_core, g_sum, g_x, g_y_out, g_y_in, g_z, g_all,
+           work, inverse, send, recv, local):
     ny, nz, block, tall = sizes
     w = lax.axis_index("wide")
     z = lax.axis_index("narrow")
     c, x, y = w % NC, (w // NC) % NX, w // (NC * NX)
     strip = tall // nz
+    half = ny // 2
+    x_left, x_right, x_far_side = (x + NX - 1) % NX, (x + 1) % NX, (x + 2) % NX
 
     def core_peer():
         return {"wide": (y * NX + x) * NC + (1 - c)}
@@ -98,6 +101,10 @@
     def z_peer(d):
         return (z + d) % nz, {"narrow": (z + d) % nz}
 
+    load_m = pltpu.make_async_copy(m_hbm, m_ref, local.at[0])
+    load_q = pltpu.make_async_copy(q_hbm, gathered.at[0, y, x, c], local.at[1])
+    load_q.start()
+    load_m.start()
     barrier = pltpu.get_barrier_semaphore()
     peers = [core_peer()] + [x_peer(d)[1] for d in range(1, NX)] + [y_peer(d)[1] for d in range(1, ny)]
     peers += [z_peer(d)[1] for d in range(1, nz)]
@@ -116,18 +123,38 @@
         return copy
 
     def gather_plane(buf, beside=None):
-        first = {d: push(buf.at[y, x, c], buf.at[y, x, c], y_peer(d)[1]) for d in far_first(ny)}
+        own = buf.at[y, x, c]
+        left, right = x_peer(NX - 1)[1], x_peer(1)[1]
+        near = sorted(range(ny), key=lambda d: min(d, ny - d))
+        from_y = {d: push(own, own, y_peer(d)[1]) for d in far_first(ny)}
+        from_left, from_right, from_far = {}, {}, {}
+
+        def spread(d):
+            slot = buf.at[(y + ny - d) % ny, x, c]
+            from_left[d] = push(slot, slot, right)
+            from_right[d] = push(slot, slot, left)
+
+        spread(0)
         if beside is not None:
             beside()
-        for d in first:
-            first[d].wait_recv()
-        second = {d: push(buf.at[:, x, c], buf.at[:, x, c], x_peer(d)[1]) for d in far_first(NX)}
-        third = [push(buf.at[:, x, c], buf.at[:, x, c], core_peer())]
-        for d in sorted(second, key=lambda d: min(d, NX - d)):
-            second[d].wait_recv()
-            came = (x + NX - d) % NX
-            third.append(push(buf.at[:, came, c], buf.at[:, came, c], core_peer()))
-        for copy in third:
+        for d in near[1:]:
+            from_y[d].wait_recv()
+            spread(d)
+        across = [push(buf.at[:, x, c], buf.at[:, x, c], core_peer())]
+        for d in near:
+            row = (y + ny - d) % ny
+            from_left[d].wait_recv()
+            if d < half:
+                from_far[d] = push(buf.at[row, x_left, c], buf.at[row, x_left, c], right)
+            from_right[d].wait_recv()
+            if d >= half:
+                from_far[d] = push(buf.at[row, x_right, c], buf.at[row, x_right, c], left)
+        for came in (x_left, x_right):
+            across.append(push(buf.at[:, came, c], buf.at[:, came, c], core_peer()))
+        for d in near:
+            from_far[d].wait_recv()
+        across.append(push(buf.at[:, x_far_side, c], buf.at[:, x_far_side, c], core_peer()))
+        for copy in across:
             copy.wait_recv()
 
     def exchange_narrow(buf):
@@ -136,6 +163,8 @@
             copy.wait_recv()
 
     def transpose_momentum():
+        load_m.wait()
+
         def one(k, carry):
             at = pl.multiple_of(k * 256, 256)
             mt[pl.ds(at, 256), :] = jnp.transpose(m_ref[:, pl.ds(at, 256)])
@@ -170,13 +199,16 @@
             copy.wait_recv()
         for d in range(1, nz):
             total = total + z_in[t, d - 1]
-        z_all[t, z] = total * scale() if scale is not None else total
-        exchange_narrow(z_all.at[t])
+        total = total * scale() if scale is not None else total
+        z_all[t, z] = total
+        return total
 
     def reduce_gram(t):
         other = pl.ds(pl.multiple_of((1 - c) * (R // NC), 8), R // NC)
         mine = pl.ds(pl.multiple_of(c * (R // NC), 8), R // NC)
-        push(g_out.at[t, other], g_core.at[t], core_peer()).wait_recv()
+        first = push(g_out.at[t, other], g_core.at[t], core_peer())
+        strips = [push(z_all.at[t, z], z_all.at[t, z], z_peer(d)[1]) for d in far_first(nz)]
+        first.wait_recv()
         g_sum[t] = (g_out[t, mine, :] + g_core[t]).reshape(NX, R // NC // NX, R)
         copies = [push(g_sum.at[t, x_peer(d)[0]], g_x.at[t, d - 1], x_peer(d)[1]) for d in far_first(NX)]
         total = g_sum[t, x]
@@ -196,6 +228,11 @@
             copy.wait_recv()
         for d in range(1, ny):
             total = total + g_y_in[t, d - 1]
+        g_z[t, z] = total
+        exchange_narrow(g_z.at[t])
+        total = g_z[t, 0]
+        for k in range(1, nz):
+            total = total + g_z[t, k]
         mine = g_all.at[t, c, x, y // 2, y % 2]
         mine[...] = total
         copies = [push(mine, mine, y_peer(d)[1]) for d in far_first(ny)]
@@ -208,35 +245,51 @@
         mine = g_all.at[t, c]
         push(mine, mine, core_peer()).wait_recv()
         halves = [g_all[t, :, :, :, h].reshape(R, R // 2) for h in range(2)]
-        return jnp.concatenate(halves, axis=1)
-
-    def back_product(t, left):
-        def one(k, carry):
-            at = pl.multiple_of(k * NX * NC * block, 256)
-            part = jnp.dot(mt[pl.ds(at, NX * NC * block), :], left, preferred_element_type=F32)
-            part = part.reshape(NX, NC, block, R)
-            partial[t, k] = part
-            partial_low[t, k] = part.astype(BF16)
-            return carry
-
-        lax.fori_loop(0, ny, one, 0)
-        order = far_first(NX) + [0]
-        first = {}
-        for d in order:
+        return jnp.concatenate(halves, axis=1), strips
+
+    def back_product(t, left_basis):
+        left, right = x_peer(NX - 1)[1], x_peer(1)[1]
+        low, high = pl.ds(0, half), pl.ds(half, half)
+        from_core = {}
+        for d in (2, 1, 3, 0):
             to = (x + d) % NX
-            first[d] = push(partial_low.at[t, :, to, 1 - c], core_in.at[t, to], core_peer())
-        second = []
-        for d in order:
+
+            def one(k, carry):
+                at = pl.multiple_of((k * NX + to) * (NC * block), NC * block)
+                part = jnp.dot(mt[pl.ds(at, NC * block), :], left_basis, preferred_element_type=F32).reshape(NC, block, R)
+                partial[t, k, to] = part
+                partial_low[t, k, to] = part.astype(BF16)
+                return carry
+
+            lax.fori_loop(0, ny, one, 0)
+            from_core[d] = push(partial_low.at[t, :, to, 1 - c], core_in.at[t, to], core_peer())
+
+        def joined(d, rows):
             to = (x + d) % NX
-            first[d].wait_recv()
-            total = partial[t, :, to, c] + core_in[t, to].astype(F32)
-            if d:
-                core_sum[t, d - 1] = total.astype(BF16)
-                second.append(push(core_sum.at[t, d - 1], x_in.at[t, d - 1], x_peer(d)[1]))
-        for copy in second:
-            copy.wait_recv()
-        for d in range(1, NX):
-            total = total + x_in[t, d - 1].astype(F32)
+            return partial[t, rows, to, c] + core_in[t, to, rows].astype(F32)
+
+        def onward(d, rows, dst, peer, extra=None):
+            total = joined(d, rows)
+            if extra is not None:
+                total = total + extra.astype(F32)
+            core_sum[t, d - 1, rows] = total.astype(BF16)
+            return push(core_sum.at[t, d - 1, rows], dst, peer)
+
+        from_core[2].wait_recv()
+        far_right = onward(2, low, x_far.at[t, 0], right)
+        far_left = onward(2, high, x_far.at[t, 1], left)
+        from_core[1].wait_recv()
+        near = [onward(1, high, x_in.at[t, 0, high], right)]
+        from_core[3].wait_recv()
+        near.append(onward(3, low, x_in.at[t, 1, low], left))
+        far_right.wait_recv()
+        near.append(onward(1, low, x_in.at[t, 0, low], right, x_far[t, 0]))
+        far_left.wait_recv()
+        near.append(onward(3, high, x_in.at[t, 1, high], left, x_far[t, 1]))
+        from_core[0].wait_recv()
+        for copy in near:
+            copy.wait_recv()
+        total = joined(0, pl.ds(0, ny)) + x_in[t, 0].astype(F32) + x_in[t, 1].astype(F32)
         x_low[t] = total.astype(BF16)
         partial[t, :, x, c] = total
         third = [push(x_low.at[t, y_peer(d)[0]], y_in.at[t, d - 1], y_peer(d)[1]) for d in far_first(ny)]
@@ -247,7 +300,7 @@
             total = total + y_in[t, d - 1].astype(F32)
         return total
 
-    gathered[0, y, x, c] = q_ref[...]
+    load_q.wait()
     gather_plane(gathered.at[0], transpose_momentum)
     for t in range(ITERS):
         z_out[t] = product(t).reshape(nz, strip, R)
@@ -260,12 +313,14 @@
                     copy.wait_recv()
                 return 1.0 / norms(t)
 
-            reduce_narrow(t, scale)
+            summed = reduce_narrow(t, scale)
         else:
-            reduce_narrow(t, None)
-        summed = z_all[t].reshape(tall, R)
+            summed = reduce_narrow(t, None)
         g_out[t] = jnp.dot(jnp.transpose(summed), summed, preferred_element_type=F32, precision=HIGHEST)
-        inverse_factor(reduce_gram(t), work, inverse)
+        gram, strips = reduce_gram(t)
+        inverse_factor(gram, work, inverse)
+        for copy in strips:
+            copy.wait_recv()
         left = dot_t(z_all[t].reshape(tall, R), inverse[...]).astype(BF16)
         right = back_product(t, left)
         gathered[t + 1, y, x, c] = right.astype(BF16)
@@ -288,8 +343,8 @@
 
 def count_copies(ny, nz):
     xs, ys, zs = NX - 1, ny - 1, nz - 1
-    gather = ys + xs + NX
-    one = zs + zs + 2 * (1 + xs + ys) + NX + xs + ys
+    gather = ys + 3 * ny + NX
+    one = 3 * zs + 2 * (1 + xs + ys) + NX + 6 + ys
     return (ITERS + 1) * gather + ITERS * one + ITERS * zs
 
 
@@ -302,13 +357,15 @@
     g_rows = R // (NC * NX * (ny // 2))
     vmem = pltpu.VMEM
     scratch = [
+        vmem((tall, broad), BF16),
         vmem((broad, tall), BF16),
         vmem((ITERS + 1, ny, NX, NC, block, R), BF16),
         vmem((ITERS, ny, NX, NC, block, R), F32),
         vmem((ITERS, ny, NX, NC, block, R), BF16),
         vmem((ITERS, NX, ny, block, R), BF16),
         vmem((ITERS, NX - 1, ny, block, R), BF16),
-        vmem((ITERS, NX - 1, ny, block, R), BF16),
+        vmem((ITERS, 2, ny // 2, block, R), BF16),
+        vmem((ITERS, 2, ny, block, R), BF16),
         vmem((ITERS, ny, block, R), BF16),
         vmem((ITERS, ny - 1, block, R), BF16),
         vmem((ITERS, nz, strip, R), F32),
@@ -321,11 +378,13 @@
         vmem((ITERS, NX - 1, R // NC // NX, R), F32),
         vmem((ITERS, ny // 2, 2, g_rows, R // 2), F32),
         vmem((ITERS, ny - 1, g_rows, R // 2), F32),
+        vmem((ITERS, nz, g_rows, R // 2), F32),
         vmem((ITERS, NC, NX, ny // 2, 2, g_rows, R // 2), F32),
         vmem((R, R), F32),
         vmem((R, R), F32),
         pltpu.SemaphoreType.DMA((copies,)),
         pltpu.SemaphoreType.DMA((copies,)),
+        pltpu.SemaphoreType.DMA((2,)),
     ]
     whole = pl.BlockSpec(memory_space=pltpu.VMEM)
     return pl.pallas_call(
@@ -336,10 +395,10 @@
             jax.ShapeDtypeStruct((8, R), F32),
             jax.ShapeDtypeStruct((block, R), BF16),
         ),
-        in_specs=[whole] * 2,
+        in_specs=[pl.BlockSpec(memory_space=pl.ANY)] * 2,
         out_specs=(whole,) * 4,
         scratch_shapes=scratch,
-        compiler_params=pltpu.CompilerParams(collective_id=0, has_side_effects=True, vmem_limit_bytes=48 * 1024 * 1024),
+        compiler_params=pltpu.CompilerParams(collective_id=0, has_side_effects=True, vmem_limit_bytes=56 * 1024 * 1024),
         name="iterate",
     )(momentum, q_rows)
 

time: 202 us -> 201 us (level)
  local copies, waits for them, and re-layouts: 4.76 us -> 0.61 us
  Pallas kernels: 196 us -> 199 us
    unnamed x11 -> x3, local copies, waits for them, and re-layouts: 4.76 us -> 0.61 us
    pallas_call x1, Pallas kernels: 192 us -> 195 us  [iterate(): pl.pallas_call(functools.partial(kernel, (ny, nz, block, tall)), out_shap...]
where the time goes in v2:
time: 201 us
  Pallas kernels  199 us (99%)
    pallas_call x1, Pallas kernels, iterate(): pl.pallas_call(functools.partial(kernel, (ny, nz, block, tall)), out_shap...  195 us
    pallas_call x1, Pallas kernels, finish(): pl.pallas_call(functools.partial(finish_kernel, scaling), grid=(broad //...  4.46 us

profile of v2, /device:TPU:1, one launch (start us, length us, event | category | flops | bytes accessed | tf_op | source)
XLA Modules:
  0.0 200.6 jit_solution(10224989386063020608)
XLA Ops:
  0.6 194.9 %iterate.1 = (bf16[256,256]{1,0:T(8,128)(2,1)}, bf16[8,256,256]{2,1,0:T(8,128)(2,1)}, f32[8,256]{1,0:T(8,128)}, bf16[32,256]{1,0:T(8,128)(2,1)}) custom-call(bf16[256,2048]{1,0:T(8,128)(2,1)} %m_ref.1, bf16[32,256]{1,0:T(8,128)(2,1)} %bitcast.4), custom_call_target="tpu_custom_call" | custom-call | tf_op jit(solution)/shard_map/iterate/pallas_call | solution.py:390
  195.5 0.0 copy-start
  195.5 4.5 %finish.1 = (f32[256,2048]{1,0:T(8,128)}, bf16[256,2048]{1,0:T(8,128)(2,1)}) custom-call(bf16[256,2048]{1,0:T(8,128)(2,1)} %m_ref.1, bf16[256,256]{1,0:T(8,128)(2,1)} %get-tuple-element.9.left_ref, bf16[2048,256]{1,0:T(8,128)(2,1)} %bitcast.3, f32[8,256]{1,0:T(8,128)} %get-tuple-element.11.norms_ref), custom_call_target="tpu_custom_call" | custom-call | tf_op jit(solution)/shard_map/finish/pallas_call | solution.py:421
  200.0 0.0 copy-done
  200.0 0.6 copy.6
Async XLA Ops:
  195.5 4.5 %copy-start = (bf16[32,256]{1,0:T(8,128)(2,1)S(1)}, bf16[32,256]{1,0:T(8,128)(2,1)}, u32[]{:S(2)}) copy-start(bf16[32,256]{1,0:T(8,128)(2,1)} %get-tuple-element.14) | copy-start | bytes 49156
